TPU v7x, 32 devices: a whole 2x2x4 slice. The times are simulated.
32 devices in a mesh: rep: 4 (over z), shard: 8 (over y, x, core).
Axes of the slice: x: 2, y: 2, z: 4, core: 2. Of those that a mesh axis runs over, the one named last changes fastest.
Arguments:
- hidden_acts: bfloat16 [4096, 1024], P(('rep', 'shard')), may hold values from -6 to 6
- out_grads: bfloat16 [4096, 8192], P(('rep', 'shard')), may hold values from -0.1875 to 0.1875
- momentum: float32 [4, 1024, 8192], P('rep', None, 'shard'), may hold values from -6 to 6
- kept: int32 [32], replicated, may hold values from 0 to 4095, as said below
Outputs:
- residual_momentum: float32 [4, 1024, 8192], P('rep', None, 'shard')
- update: bfloat16 [1024, 8192], P(None, 'shard')
Inputs may be any that keep to these rules, and one draw needn't show every extreme that they name: `kept`: 32 distinct indices u * 64 + v of a block's coefficients, u the row frequency and v the column frequency; the same list for every block.
All inputs are finite; a program needn't handle non-finite values.
Results may differ from a plain program's by a relative error of at most 0.001.
Values may be sent and summed in bfloat16 or wider, within the bound.
A program may use at most 128 MiB of HBM per device.

v0:
```python
import functools
import math

import jax
import jax.numpy as jnp
import numpy as np
from jax import lax
from jax.experimental import pallas as pl
from jax.experimental.pallas import tpu as pltpu
from jax.sharding import PartitionSpec as P

GROUP = 64
WIDTH = 256
DECAY = 0.9
MESH = pl.DeviceIdType.MESH


def cosine_matrix(length):
    frequency = np.arange(length, dtype=np.float64)[:, None]
    position = np.arange(length, dtype=np.float64)[None, :]
    cosines = np.cos(math.pi * (2.0 * position + 1.0) * frequency / (2.0 * length)) * math.sqrt(2.0 / length)
    return (cosines * np.where(frequency == 0.0, math.sqrt(0.5), 1.0)).astype(np.float32)


def flip(index, bits):
    out = index
    power = 1
    while power <= bits:
        if bits & power:
            out = out + power - 2 * power * ((index // power) % 2)
        power *= 2
    return out


def split(x):
    high = x.astype(jnp.bfloat16)
    return high, (x - high.astype(jnp.float32)).astype(jnp.bfloat16)


def dot_nt(a, b):
    return lax.dot_general(a, b, (((1,), (1,)), ((), ())), preferred_element_type=jnp.float32)


def dot_nn(a, b):
    return lax.dot_general(a, b, (((1,), (0,)), ((), ())), preferred_element_type=jnp.float32)


def exchange_kernel(
    shards, reps, chunks, kept_count,
    kept_ref, cos_t_ref, cos_tiled_ref, acts_ref, grads_ref, momentum_ref,
    fresh_ref, coeffs_ref, total_ref, right_ref, left_ref,
    own_acts, acts_t, grads_all, fresh, gathered,
    acts_send, acts_recv, grads_send, grads_recv, rep_send, rep_recv,
    local_acts, local_grads, local_mom, out_sem,
):
    rep = lax.axis_index("rep")
    me = lax.axis_index("shard")
    sibling = flip(me, 1)
    tok, rows = acts_ref.shape
    columns = chunks * WIDTH
    tiles = WIDTH // GROUP
    lanes = tiles * kept_count

    pltpu.make_async_copy(acts_ref, own_acts, local_acts).start()

    def own_grads(j):
        return pltpu.make_async_copy(
            grads_ref.at[:, pl.ds(pl.multiple_of(me * columns + j * WIDTH, WIDTH), WIDTH)],
            grads_all.at[j, pl.ds(0, tok), :],
            local_grads.at[j],
        )

    def load_momentum(j):
        return pltpu.make_async_copy(
            momentum_ref.at[0, :, pl.ds(pl.multiple_of(j * WIDTH, WIDTH), WIDTH)], fresh.at[j], local_mom.at[j]
        )

    def store_fresh(j):
        return pltpu.make_async_copy(
            fresh.at[j], fresh_ref.at[:, pl.ds(pl.multiple_of(j * WIDTH, WIDTH), WIDTH)], out_sem.at[j]
        )

    barrier = pltpu.get_barrier_semaphore()
    for o in range(1, shards):
        pl.semaphore_signal(barrier, inc=1, device_id=(rep, flip(me, o)), device_id_type=MESH)
    for q in range(1, reps):
        pl.semaphore_signal(barrier, inc=1, device_id=(flip(rep, q), me), device_id_type=MESH)

    def send_grads(o, j):
        peer = flip(me, o)
        return pltpu.make_async_remote_copy(
            src_ref=grads_ref.at[:, pl.ds(pl.multiple_of(peer * columns + j * WIDTH, WIDTH), WIDTH)],
            dst_ref=grads_all.at[j, pl.ds(o * tok, tok), :],
            send_sem=grads_send.at[j, o],
            recv_sem=grads_recv.at[j, o],
            device_id=(rep, peer),
            device_id_type=MESH,
        )

    def acts_slot(o):
        return acts_t.at[:, pl.ds(o * tok, tok)]

    def send_acts(o):
        source = acts_slot(0 if o % 2 == 0 else o - 1)
        peer = flip(me, o) if o % 2 == 0 else sibling
        return pltpu.make_async_remote_copy(
            src_ref=source,
            dst_ref=acts_slot(o),
            send_sem=acts_send.at[o],
            recv_sem=acts_recv.at[o],
            device_id=(rep, peer),
            device_id_type=MESH,
        )

    def send_coeffs(q, j):
        return pltpu.make_async_remote_copy(
            src_ref=coeffs_ref.at[j],
            dst_ref=gathered.at[j, q],
            send_sem=rep_send.at[j, q],
            recv_sem=rep_recv.at[j, q],
            device_id=(flip(rep, q), me),
            device_id_type=MESH,
        )

    pltpu.make_async_copy(acts_ref, own_acts, local_acts).wait()
    acts_t[:, pl.ds(0, tok)] = own_acts[...].T
    pl.semaphore_wait(barrier, shards - 1 + reps - 1)

    for o in range(shards - 2, 1, -2):
        send_acts(o).start()
    send_acts(1).start()
    for j in range(chunks):
        for o in range(shards - 1, 0, -1):
            send_grads(o, j).start()
    for j in range(chunks):
        own_grads(j).start()
        load_momentum(j).start()

    row = lax.broadcasted_iota(jnp.int32, (lanes, GROUP), 0) % kept_count
    freq_v = lax.broadcasted_iota(jnp.int32, (lanes, GROUP), 1)
    lane = lax.broadcasted_iota(jnp.int32, (GROUP, lanes), 1) % kept_count
    freq_u = lax.broadcasted_iota(jnp.int32, (GROUP, lanes), 0)
    hot_v = jnp.zeros((lanes, GROUP), jnp.float32)
    hot_u = jnp.zeros((GROUP, lanes), jnp.float32)
    for k in range(kept_count):
        index = kept_ref[k]
        hot_v = jnp.where((row == k) & (freq_v == index % GROUP), 1.0, hot_v)
        hot_u = jnp.where((lane == k) & (freq_u == index // GROUP), 1.0, hot_u)
    right = jnp.dot(
        hot_v, cos_tiled_ref[...], precision=lax.Precision.HIGHEST, preferred_element_type=jnp.float32
    )
    same_tile = (
        lax.broadcasted_iota(jnp.int32, (lanes, WIDTH), 0) // kept_count
        == lax.broadcasted_iota(jnp.int32, (lanes, WIDTH), 1) // GROUP
    )
    right_ref[...] = jnp.where(same_tile, right, 0.0)
    left_ref[...] = jnp.dot(
        cos_t_ref[...], hot_u, precision=lax.Precision.HIGHEST, preferred_element_type=jnp.float32
    )

    for o in range(2, shards, 2):
        send_acts(o).wait_recv()
        send_acts(o + 1).start()
    for o in range(1, shards, 2):
        send_acts(o).wait_recv()

    half = rows // 2
    bands = half // GROUP

    def chunk(j, carry):
        for o in range(1, shards):
            send_grads(o, j).wait_recv()
        own_grads(j).wait()
        load_momentum(j).wait()
        right_high, right_low = split(right_ref[...])
        right_both = jnp.concatenate([right_high, right_low], axis=0)
        left = left_ref[...]
        for t in range(2):
            part = pl.ds(t * half, half)
            gradient = dot_nn(acts_t[part, :], grads_all[j])
            value = DECAY * fresh[j, part, :] + gradient
            fresh[j, part, :] = value
            high, low = split(value)
            both = dot_nt(high, right_both)
            done = both[:, :lanes] + both[:, lanes:] + dot_nt(low, right_high)
            coeffs_ref[j, pl.ds(t * bands, bands), :] = jnp.sum(
                done.reshape(bands, GROUP, lanes) * left[None], axis=1
            )
        for q in range(1, reps):
            send_coeffs(q, j).start()
        store_fresh(j).start()
        return carry

    lax.fori_loop(0, chunks, chunk, 0)

    def finish(j, carry):
        for q in range(1, reps):
            send_coeffs(q, j).wait_recv()
        terms = [coeffs_ref[j]] + [gathered[j, q] for q in range(1, reps)]
        while len(terms) > 1:
            terms = [terms[i] + terms[i + 1] for i in range(0, len(terms), 2)]
        total_ref[j] = terms[0]
        for q in range(1, reps):
            send_coeffs(q, j).wait_send()
        for o in range(1, shards):
            send_grads(o, j).wait_send()
        store_fresh(j).wait()
        return carry

    lax.fori_loop(0, chunks, finish, 0)
    for o in range(1, shards):
        send_acts(o).wait_send()


def decode_kernel(fresh_ref, coeffs_ref, total_ref, right_ref, left_ref, residual_ref, update_ref):
    right_high, right_low = split(right_ref[...])
    twice = jnp.concatenate([right_high, right_high], axis=0)
    left = left_ref[...]
    rows = fresh_ref.shape[0]
    lanes = left.shape[1]
    bands = rows // GROUP

    def decode(values):
        dense = (values[:, None, :] * left[None]).reshape(rows, lanes)
        high, low = split(dense)
        return dot_nn(jnp.concatenate([high, low], axis=1), twice) + dot_nn(high, right_low)

    residual_ref[0] = fresh_ref[...] - decode(coeffs_ref[0])
    update_ref[...] = decode(total_ref[0]).astype(jnp.bfloat16)


def on_device(shards, reps, hidden_acts, out_grads, momentum, kept):
    tok, rows = hidden_acts.shape
    columns = momentum.shape[2]
    chunks = columns // WIDTH
    kept_count = kept.shape[0]
    tiles = WIDTH // GROUP
    lanes = tiles * kept_count
    bands = rows // GROUP
    cosines = cosine_matrix(GROUP)
    f32 = jnp.float32
    any_space = pl.BlockSpec(memory_space=pl.ANY)
    vmem = pl.BlockSpec(memory_space=pltpu.VMEM)
    fresh, coeffs, total, right, left = pl.pallas_call(
        functools.partial(exchange_kernel, shards, reps, chunks, kept_count),
        out_shape=(
            jax.ShapeDtypeStruct((rows, columns), f32),
            jax.ShapeDtypeStruct((chunks, bands, lanes), f32),
            jax.ShapeDtypeStruct((chunks, bands, lanes), f32),
            jax.ShapeDtypeStruct((lanes, WIDTH), f32),
            jax.ShapeDtypeStruct((GROUP, lanes), f32),
        ),
        in_specs=[pl.BlockSpec(memory_space=pltpu.SMEM), vmem, vmem, any_space, any_space, any_space],
        out_specs=(any_space, vmem, vmem, vmem, vmem),
        scratch_shapes=[
            pltpu.VMEM((tok, rows), jnp.bfloat16),
            pltpu.VMEM((rows, shards * tok), jnp.bfloat16),
            pltpu.VMEM((chunks, shards * tok, WIDTH), jnp.bfloat16),
            pltpu.VMEM((chunks, rows, WIDTH), f32),
            pltpu.VMEM((chunks, reps, bands, lanes), f32),
            pltpu.SemaphoreType.DMA((shards,)),
            pltpu.SemaphoreType.DMA((shards,)),
            pltpu.SemaphoreType.DMA((chunks, shards)),
            pltpu.SemaphoreType.DMA((chunks, shards)),
            pltpu.SemaphoreType.DMA((chunks, reps)),
            pltpu.SemaphoreType.DMA((chunks, reps)),
            pltpu.SemaphoreType.DMA,
            pltpu.SemaphoreType.DMA((chunks,)),
            pltpu.SemaphoreType.DMA((chunks,)),
            pltpu.SemaphoreType.DMA((chunks,)),
        ],
        compiler_params=pltpu.CompilerParams(
            collective_id=0, has_side_effects=True, vmem_limit_bytes=48 * 2**20
        ),
        name="exchange",
    )(
        kept,
        jnp.asarray(np.ascontiguousarray(cosines.T)),
        jnp.asarray(np.tile(cosines, (1, tiles))),
        hidden_acts,
        out_grads,
        momentum,
    )
    residual, update = pl.pallas_call(
        decode_kernel,
        grid=(2, chunks),
        out_shape=(
            jax.ShapeDtypeStruct((1, rows, columns), f32),
            jax.ShapeDtypeStruct((rows, columns), jnp.bfloat16),
        ),
        in_specs=[
            pl.BlockSpec((rows // 2, WIDTH), lambda i, j: (i, j)),
            pl.BlockSpec((1, bands // 2, lanes), lambda i, j: (j, i, 0)),
            pl.BlockSpec((1, bands // 2, lanes), lambda i, j: (j, i, 0)),
            pl.BlockSpec((lanes, WIDTH), lambda i, j: (0, 0)),
            pl.BlockSpec((GROUP, lanes), lambda i, j: (0, 0)),
        ],
        out_specs=(
            pl.BlockSpec((1, rows // 2, WIDTH), lambda i, j: (0, i, j)),
            pl.BlockSpec((rows // 2, WIDTH), lambda i, j: (i, j)),
        ),
        compiler_params=pltpu.CompilerParams(vmem_limit_bytes=32 * 2**20),
        name="decode",
    )(fresh, coeffs, total, right, left)
    return residual, update


def solution(mesh):
    placed = (P(("rep", "shard"), None), P(("rep", "shard"), None), P("rep", None, "shard"), P())
    return jax.shard_map(
        functools.partial(on_device, mesh.shape["shard"], mesh.shape["rep"]),
        mesh=mesh,
        in_specs=placed,
        out_specs=(P("rep", None, "shard"), P(None, "shard")),
        check_vma=False,
    )
```

profile of v0, /device:TPU:0, one launch (start us, length us, event | category | flops | bytes accessed | tf_op | source)
XLA Modules:
  0.0 61.9 jit_solution(16299462780742910042)
XLA Ops:
  0.6 0.0 copy-start.1
  0.6 1.6 %copy-done.1 = bf16[128,8192]{1,0:T(8,128)(2,1)S(1)} copy-done((bf16[128,8192]{1,0:T(8,128)(2,1)S(1)}, bf16[128,8192]{1,0:T(8,128)(2,1)}, u32[]{:S(2)}) %copy-start.1) | copy-done | bytes 2097176
  2.2 0.0 copy-start.2
  2.2 0.9 %copy-done.2 = bf16[128,1024]{1,0:T(8,128)(2,1)S(1)} copy-done((bf16[128,1024]{1,0:T(8,128)(2,1)S(1)}, bf16[128,1024]{1,0:T(8,128)(2,1)}, u32[]{:S(2)}) %copy-start.2) | copy-done | bytes 262168
  3.2 0.0 copy-start.3
  3.2 0.8 %copy-done.3 = f32[64,256]{1,0:T(8,128)S(1)} copy-done((f32[64,256]{1,0:T(8,128)S(1)}, f32[64,256]{1,0:T(8,128)}, u32[]{:S(2)}) %copy-start.3) | copy-done | bytes 65560
  4.0 0.0 copy-start.4
  4.0 0.8 %copy-done.4 = f32[64,64]{1,0:T(8,128)S(1)} copy-done((f32[64,64]{1,0:T(8,128)S(1)}, f32[64,64]{1,0:T(8,128)}, u32[]{:S(2)}) %copy-start.4) | copy-done | bytes 16408
  4.8 0.0 copy-start.5
  4.8 0.7 %copy-done.5 = s32[32]{0:T(128)S(1)} copy-done((s32[32]{0:T(128)S(1)}, s32[32]{0:T(128)}, u32[]{:S(2)}) %copy-start.5) | copy-done | bytes 152
  5.4 48.3 %exchange.1 = (f32[1024,1024]{1,0:T(8,128)}, f32[4,16,128]{2,1,0:T(8,128)S(1)}, f32[4,16,128]{2,1,0:T(8,128)S(1)}, f32[128,256]{1,0:T(8,128)S(1)}, f32[64,128]{1,0:T(8,128)S(1)}) custom-call(s32[32]{0:T(128)S(1)} %copy-done.5, f32[64,64]{1,0:T(8,128)S(1)} %copy-done.4, f32[64,256]{1,0:T(8,128)S(1)} %copy-done.3, bf16[128,1024]{1,0:T(8,128)(2,1)S(1)} %copy-done.2, ...), custom_call_target="tpu_custom_call" | custom-call | tf_op jit(solution)/shard_map/exchange/pallas_call | solution.py:244
  53.7 0.0 copy-start
  53.8 2.2 %copy-done = f32[1024,1024]{1,0:T(8,128)S(1)} copy-done((f32[1024,1024]{1,0:T(8,128)S(1)}, f32[1024,1024]{1,0:T(8,128)}, u32[]{:S(2)}) %copy-start) | copy-done | bytes 4194328
  55.9 5.9 %decode.1 = (f32[1,1024,1024]{2,1,0:T(8,128)}, bf16[1024,1024]{1,0:T(8,128)(2,1)}) custom-call(f32[1024,1024]{1,0:T(8,128)S(1)} %copy-done, f32[4,16,128]{2,1,0:T(8,128)S(1)} %get-tuple-element.8.coeffs_ref, f32[4,16,128]{2,1,0:T(8,128)S(1)} %get-tuple-element.9.total_ref, f32[128,256]{1,0:T(8,128)S(1)} %get-tuple-element.10.right_ref, ...), custom_call_target="tpu_custom_call" | custom-call | tf_op jit(solution)/shard_map/decode/pallas_call | solution.py:284
Async XLA Ops:
  0.6 1.6 %copy-start.1 = (bf16[128,8192]{1,0:T(8,128)(2,1)S(1)}, bf16[128,8192]{1,0:T(8,128)(2,1)}, u32[]{:S(2)}) copy-start(bf16[128,8192]{1,0:T(8,128)(2,1)} %grads_ref.1) | copy-start | bytes 6291460
  2.2 0.9 %copy-start.2 = (bf16[128,1024]{1,0:T(8,128)(2,1)S(1)}, bf16[128,1024]{1,0:T(8,128)(2,1)}, u32[]{:S(2)}) copy-start(bf16[128,1024]{1,0:T(8,128)(2,1)} %acts_ref.1) | copy-start | bytes 786436
  3.2 0.8 %copy-start.3 = (f32[64,256]{1,0:T(8,128)S(1)}, f32[64,256]{1,0:T(8,128)}, u32[]{:S(2)}) copy-start(f32[64,256]{1,0:T(8,128)} %constant.5.clone.cos_tiled_ref) | copy-start | bytes 196612
  4.0 0.8 %copy-start.4 = (f32[64,64]{1,0:T(8,128)S(1)}, f32[64,64]{1,0:T(8,128)}, u32[]{:S(2)}) copy-start(f32[64,64]{1,0:T(8,128)} %constant.4.clone.cos_t_ref) | copy-start | bytes 49156
  4.8 0.7 %copy-start.5 = (s32[32]{0:T(128)S(1)}, s32[32]{0:T(128)}, u32[]{:S(2)}) copy-start(s32[32]{0:T(128)} %kept_ref.1) | copy-start | bytes 388
  53.7 2.2 %copy-start = (f32[1024,1024]{1,0:T(8,128)S(1)}, f32[1024,1024]{1,0:T(8,128)}, u32[]{:S(2)}) copy-start(f32[1024,1024]{1,0:T(8,128)} %get-tuple-element.7.fresh_ref) | copy-start | bytes 12582916
where the time goes:
time: 62.2 us; the launch traced here: 61.9 us
  Pallas kernels  54.2 us (87%)
  local copies, waits for them, and re-layouts  6.97 us (11%)
  between operations  0.66 us (1%)
    pallas_call x1, Pallas kernels, on_device(): pl.pallas_call(functools.partial(exchange_kernel, shards, reps, chunks, k...  48.3 us
    unnamed x12, local copies, waits for them, and re-layouts  6.97 us
    pallas_call x1, Pallas kernels, on_device(): pl.pallas_call(decode_kernel, grid=(2, chunks), out_shape=(jax.ShapeDtype...  5.94 us

commit v1 on v0

v1 whole, which is shorter than its diff:
```python
import functools
import math

import jax
import jax.numpy as jnp
import numpy as np
from jax import lax
from jax.experimental import pallas as pl
from jax.experimental.pallas import tpu as pltpu
from jax.sharding import PartitionSpec as P

GROUP = 64
WIDTH = 256
DECAY = 0.9
MESH = pl.DeviceIdType.MESH


def cosine_matrix(length):
    frequency = np.arange(length, dtype=np.float64)[:, None]
    position = np.arange(length, dtype=np.float64)[None, :]
    cosines = np.cos(math.pi * (2.0 * position + 1.0) * frequency / (2.0 * length)) * math.sqrt(2.0 / length)
    return (cosines * np.where(frequency == 0.0, math.sqrt(0.5), 1.0)).astype(np.float32)


def flip(index, bits):
    out = index
    power = 1
    while power <= bits:
        if bits & power:
            out = out + power - 2 * power * ((index // power) % 2)
        power *= 2
    return out


def split(x):
    high = x.astype(jnp.bfloat16)
    return high, (x - high.astype(jnp.float32)).astype(jnp.bfloat16)


def dot_nt(a, b):
    return lax.dot_general(a, b, (((1,), (1,)), ((), ())), preferred_element_type=jnp.float32)


def dot_nn(a, b):
    return lax.dot_general(a, b, (((1,), (0,)), ((), ())), preferred_element_type=jnp.float32)


def decode(values, left, right_high, right_low):
    bands, lanes = values.shape
    dense = (values[:, None, :] * left[None]).reshape(bands * GROUP, lanes)
    high, low = split(dense)
    twice = jnp.concatenate([right_high, right_high], axis=0)
    return dot_nn(jnp.concatenate([high, low], axis=1), twice) + dot_nn(high, right_low)


def exchange_kernel(
    shards, reps, chunks, kept_count,
    kept_hbm, table_hbm, acts_ref, grads_ref, momentum_ref,
    residual_ref, update_ref, total_ref, right_ref, left_ref,
    kept_ref, table, own_acts, acts_t, grads_all, coeffs, gathered,
    acts_send, acts_recv, grads_send, grads_recv, rep_send, rep_recv,
    local_kept, local_table, local_acts, local_grads, local_mom,
):
    rep = lax.axis_index("rep")
    me = lax.axis_index("shard")
    core = me % 2
    tok, rows = acts_ref.shape
    columns = chunks * WIDTH
    tiles = WIDTH // GROUP
    lanes = tiles * kept_count
    chips = shards // 2
    square = chips == 4
    offsets = sorted(range(1, chips), key=lambda c: c == 2)

    load_acts = pltpu.make_async_copy(acts_ref, own_acts, local_acts)
    load_kept = pltpu.make_async_copy(kept_hbm, kept_ref, local_kept)
    load_table = pltpu.make_async_copy(table_hbm, table, local_table)
    load_acts.start()

    barrier = pltpu.get_barrier_semaphore()
    for o in range(1, shards):
        pl.semaphore_signal(barrier, inc=1, device_id=(rep, flip(me, o)), device_id_type=MESH)
    for q in range(1, reps):
        pl.semaphore_signal(barrier, inc=1, device_id=(flip(rep, q), me), device_id_type=MESH)
    load_kept.start()
    load_table.start()

    def own_grads(j):
        return pltpu.make_async_copy(
            grads_ref.at[:, pl.ds(pl.multiple_of(me * columns + j * WIDTH, WIDTH), WIDTH)],
            grads_all.at[j, pl.ds(0, tok), :],
            local_grads.at[j],
        )

    def load_momentum(j):
        return pltpu.make_async_copy(
            momentum_ref.at[0, :, pl.ds(pl.multiple_of(j * WIDTH, WIDTH), WIDTH)],
            residual_ref.at[j],
            local_mom.at[j],
        )

    def send_grads(o, j):
        peer = flip(me, o)
        return pltpu.make_async_remote_copy(
            src_ref=grads_ref.at[:, pl.ds(pl.multiple_of(peer * columns + j * WIDTH, WIDTH), WIDTH)],
            dst_ref=grads_all.at[j, pl.ds(o * tok, tok), :],
            send_sem=grads_send.at[j, o],
            recv_sem=grads_recv.at[j, o],
            device_id=(rep, peer),
            device_id_type=MESH,
        )

    def start_grads(j):
        for own, order in ((0, offsets), (1, offsets[::-1])):
            @pl.when(core == own)
            def _():
                for c in order:
                    send_grads(2 * c, j).start()
                    send_grads(2 * c + 1, j).start()
                send_grads(1, j).start()

    def acts_copy(source, slot, bits, low, count, sem):
        return pltpu.make_async_remote_copy(
            src_ref=acts_t.at[pl.ds(low, count), pl.ds(source * tok, tok)],
            dst_ref=acts_t.at[pl.ds(low, count), pl.ds(slot * tok, tok)],
            send_sem=acts_send.at[sem],
            recv_sem=acts_recv.at[sem],
            device_id=(rep, flip(me, bits)),
            device_id_type=MESH,
        )

    def send_direct(o):
        return acts_copy(0, o, o, 0, rows, o)

    def send_sibling(o):
        return acts_copy(o, o + 1, 1, 0, rows, o + 1)

    def send_across(bits):
        if bits == 2:
            return acts_copy(4, 6, 2, rows // 2, rows // 2, shards)
        return acts_copy(2, 6, 4, 0, rows // 2, 6)

    def send_coeffs(q, j):
        return pltpu.make_async_remote_copy(
            src_ref=coeffs.at[j],
            dst_ref=gathered.at[j, q],
            send_sem=rep_send.at[j, q],
            recv_sem=rep_recv.at[j, q],
            device_id=(flip(rep, q), me),
            device_id_type=MESH,
        )

    load_acts.wait()
    acts_t[:, pl.ds(0, tok)] = own_acts[...].T
    pl.semaphore_wait(barrier, shards - 1 + reps - 1)

    direct = [c for c in offsets if not (square and c == 3)]
    for own, order in ((0, direct), (1, direct[::-1])):
        @pl.when(core == own)
        def _():
            for c in order:
                send_direct(2 * c).start()
    send_sibling(0).start()
    start_grads(0)
    for j in range(chunks):
        own_grads(j).start()
        load_momentum(j).start()

    load_kept.wait()
    load_table.wait()
    row = lax.broadcasted_iota(jnp.int32, (lanes, GROUP), 0) % kept_count
    freq_v = lax.broadcasted_iota(jnp.int32, (lanes, GROUP), 1)
    lane = lax.broadcasted_iota(jnp.int32, (GROUP, lanes), 1) % kept_count
    freq_u = lax.broadcasted_iota(jnp.int32, (GROUP, lanes), 0)
    hot_v = jnp.zeros((lanes, GROUP), jnp.float32)
    hot_u = jnp.zeros((GROUP, lanes), jnp.float32)
    for k in range(kept_count):
        index = kept_ref[k]
        hot_v = jnp.where((row == k) & (freq_v == index % GROUP), 1.0, hot_v)
        hot_u = jnp.where((lane == k) & (freq_u == index // GROUP), 1.0, hot_u)
    right = jnp.dot(
        hot_v, table[:, :WIDTH], precision=lax.Precision.HIGHEST, preferred_element_type=jnp.float32
    )
    same_tile = (
        lax.broadcasted_iota(jnp.int32, (lanes, WIDTH), 0) // kept_count
        == lax.broadcasted_iota(jnp.int32, (lanes, WIDTH), 1) // GROUP
    )
    right_ref[...] = jnp.where(same_tile, right, 0.0)
    left_ref[...] = jnp.dot(
        table[:, WIDTH:WIDTH + GROUP], hot_u, precision=lax.Precision.HIGHEST, preferred_element_type=jnp.float32
    )

    for own, order in ((0, direct), (1, direct[::-1])):
        @pl.when(core == own)
        def _():
            for c in order:
                send_direct(2 * c).wait_recv()
                if square:
                    send_across(6 - 2 * c).start()
                send_sibling(2 * c).start()
    ahead = min(3, chunks)
    for j in range(1, min(2, chunks)):
        start_grads(j)
    if square:
        send_across(4).wait_recv()
        send_across(2).wait_recv()
        send_sibling(6).start()
    for j in range(2, ahead):
        start_grads(j)
    for o in range(0, shards, 2):
        send_sibling(o).wait_recv()

    half = rows // 2
    bands = half // GROUP

    def finish(j, with_update):
        for q in range(1, reps):
            send_coeffs(q, j).wait_recv()
        terms = [coeffs[j]] + [gathered[j, q] for q in range(1, reps)]
        while len(terms) > 1:
            terms = [terms[i] + terms[i + 1] for i in range(0, len(terms), 2)]
        total_ref[...] = terms[0]
        if with_update:
            right_high, right_low = split(right_ref[...])
            for t in range(2):
                values = total_ref[pl.ds(t * bands, bands), :]
                update_ref[j, pl.ds(t * half, half), :] = decode(
                    values, left_ref[...], right_high, right_low
                ).astype(jnp.bfloat16)

    def chunk(j, carry):
        for o in range(1, shards):
            send_grads(o, j).wait_recv()

        @pl.when(j + ahead < chunks)
        def _():
            start_grads(j + ahead)

        own_grads(j).wait()
        load_momentum(j).wait()
        right_high, right_low = split(right_ref[...])
        right_both = jnp.concatenate([right_high, right_low], axis=0)
        left = left_ref[...]
        for t in range(2):
            part = pl.ds(t * half, half)
            gradient = dot_nn(acts_t[part, :], grads_all[j])
            value = DECAY * residual_ref[j, part, :] + gradient
            residual_ref[j, part, :] = value
            high, low = split(value)
            both = dot_nt(high, right_both)
            done = both[:, :lanes] + both[:, lanes:] + dot_nt(low, right_high)
            coeffs[j, pl.ds(t * bands, bands), :] = jnp.sum(
                done.reshape(bands, GROUP, lanes) * left[None], axis=1
            )
        for q in range(1, reps):
            send_coeffs(q, j).start()
        for t in range(2):
            part = pl.ds(t * half, half)
            values = coeffs[j, pl.ds(t * bands, bands), :]
            residual_ref[j, part, :] = residual_ref[j, part, :] - decode(values, left, right_high, right_low)

        @pl.when(j > 0)
        def _():
            finish(j - 1, True)

        return carry

    lax.fori_loop(0, chunks, chunk, 0)

    def drain(j, carry):
        for o in range(1, shards):
            send_grads(o, j).wait_send()
        return carry

    lax.fori_loop(0, chunks, drain, 0)
    for c in direct:
        send_direct(2 * c).wait_send()
    for o in range(0, shards, 2):
        send_sibling(o).wait_send()
    if square:
        send_across(2).wait_send()
        send_across(4).wait_send()
    finish(chunks - 1, False)
    for j in range(chunks):
        for q in range(1, reps):
            send_coeffs(q, j).wait_send()


def store_kernel(
    residual_ref, update_ref, total_ref, right_ref, left_ref, residual_out, update_out, last, residual_sem, update_sem
):
    chunks, rows, _ = residual_ref.shape

    def store(source, target, sem, j):
        return pltpu.make_async_copy(source, target.at[:, pl.ds(j * WIDTH, WIDTH)], sem.at[j])

    copies = [store(update_ref.at[j], update_out, update_sem, j) for j in range(chunks - 1)]
    copies += [store(residual_ref.at[j], residual_out.at[0], residual_sem, j) for j in range(chunks)]
    for copy in copies:
        copy.start()
    right_high, right_low = split(right_ref[...])
    last[...] = decode(total_ref[...], left_ref[...], right_high, right_low).astype(jnp.bfloat16)
    copies.append(store(last, update_out, update_sem, chunks - 1))
    copies[-1].start()
    for copy in copies:
        copy.wait()


def on_device(shards, reps, hidden_acts, out_grads, momentum, kept):
    tok, rows = hidden_acts.shape
    columns = momentum.shape[2]
    chunks = columns // WIDTH
    kept_count = kept.shape[0]
    tiles = WIDTH // GROUP
    lanes = tiles * kept_count
    bands = rows // GROUP
    cosines = cosine_matrix(GROUP)
    table = np.concatenate(
        [np.tile(cosines, (1, tiles)), cosines.T, np.zeros((GROUP, 128 - GROUP), np.float32)], axis=1
    )
    f32 = jnp.float32
    hbm = pl.BlockSpec(memory_space=pltpu.HBM)
    vmem = pl.BlockSpec(memory_space=pltpu.VMEM)
    in_hbm = functools.partial(pltpu.with_memory_space_constraint, memory_space=pltpu.HBM)
    kept_parts = pl.pallas_call(
        functools.partial(exchange_kernel, shards, reps, chunks, kept_count),
        out_shape=(
            jax.ShapeDtypeStruct((chunks, rows, WIDTH), f32),
            jax.ShapeDtypeStruct((chunks, rows, WIDTH), jnp.bfloat16),
            jax.ShapeDtypeStruct((bands, lanes), f32),
            jax.ShapeDtypeStruct((lanes, WIDTH), f32),
            jax.ShapeDtypeStruct((GROUP, lanes), f32),
        ),
        in_specs=[hbm] * 5,
        out_specs=(vmem,) * 5,
        scratch_shapes=[
            pltpu.SMEM((kept_count,), jnp.int32),
            pltpu.VMEM(table.shape, f32),
            pltpu.VMEM((tok, rows), jnp.bfloat16),
            pltpu.VMEM((rows, shards * tok), jnp.bfloat16),
            pltpu.VMEM((chunks, shards * tok, WIDTH), jnp.bfloat16),
            pltpu.VMEM((chunks, bands, lanes), f32),
            pltpu.VMEM((chunks, reps, bands, lanes), f32),
            pltpu.SemaphoreType.DMA((shards + 1,)),
            pltpu.SemaphoreType.DMA((shards + 1,)),
            pltpu.SemaphoreType.DMA((chunks, shards)),
            pltpu.SemaphoreType.DMA((chunks, shards)),
            pltpu.SemaphoreType.DMA((chunks, reps)),
            pltpu.SemaphoreType.DMA((chunks, reps)),
            pltpu.SemaphoreType.DMA,
            pltpu.SemaphoreType.DMA,
            pltpu.SemaphoreType.DMA,
            pltpu.SemaphoreType.DMA((chunks,)),
            pltpu.SemaphoreType.DMA((chunks,)),
        ],
        compiler_params=pltpu.CompilerParams(
            collective_id=0, has_side_effects=True, vmem_limit_bytes=40 * 2**20
        ),
        name="exchange",
    )(*(in_hbm(x) for x in (kept, jnp.asarray(table), hidden_acts, out_grads, momentum)))
    return pl.pallas_call(
        store_kernel,
        out_shape=(
            jax.ShapeDtypeStruct((1, rows, columns), f32),
            jax.ShapeDtypeStruct((rows, columns), jnp.bfloat16),
        ),
        in_specs=[vmem] * 5,
        out_specs=(hbm, hbm),
        scratch_shapes=[
            pltpu.VMEM((rows, WIDTH), jnp.bfloat16),
            pltpu.SemaphoreType.DMA((chunks,)),
            pltpu.SemaphoreType.DMA((chunks,)),
        ],
        compiler_params=pltpu.CompilerParams(vmem_limit_bytes=24 * 2**20),
        name="store",
    )(*kept_parts)


def solution(mesh):
    placed = (P(("rep", "shard"), None), P(("rep", "shard"), None), P("rep", None, "shard"), P())
    return jax.shard_map(
        functools.partial(on_device, mesh.shape["shard"], mesh.shape["rep"]),
        mesh=mesh,
        in_specs=placed,
        out_specs=(P("rep", None, "shard"), P(None, "shard")),
        check_vma=False,
    )
```

time: 62.2 us -> 48 us (0.77)
  Pallas kernels: 54.2 us -> 47.2 us
  local copies, waits for them, and re-layouts: 6.97 us -> 0 us
    unnamed x12 -> x0, local copies, waits for them, and re-layouts: 6.97 us -> none
    pallas_call x1, Pallas kernels: 48.3 us -> 44.5 us  [on_device(): pl.pallas_call(functools.partial(exchange_kernel, shards, reps, chunks, k...]
    pallas_call x1, Pallas kernels: 5.94 us -> 2.74 us  [on_device(): pl.pallas_call(store_kernel, out_shape=(jax.ShapeDtypeStruct((1, rows, co...]
where the time goes in v1:
time: 48 us; the launch traced here: 47.8 us
  Pallas kernels  47.2 us (98%)
  between operations  0.64 us (1%)
    pallas_call x1, Pallas kernels, on_device(): pl.pallas_call(functools.partial(exchange_kernel, shards, reps, chunks, k...  44.5 us
    pallas_call x1, Pallas kernels, on_device(): pl.pallas_call(store_kernel, out_shape=(jax.ShapeDtypeStruct((1, rows, co...  2.74 us

profile of v1, /device:TPU:0, one launch (start us, length us, event | category | flops | bytes accessed | tf_op | source)
XLA Modules:
  0.0 47.8 jit_solution(8266350198434713464)
XLA Ops:
  0.6 44.5 %exchange.1 = (f32[4,1024,256]{2,1,0:T(8,128)S(1)}, bf16[4,1024,256]{2,1,0:T(8,128)(2,1)S(1)}, f32[16,128]{1,0:T(8,128)S(1)}, f32[128,256]{1,0:T(8,128)S(1)}, f32[64,128]{1,0:T(8,128)S(1)}) custom-call(s32[32]{0:T(128)} %kept_hbm.1, f32[64,384]{1,0:T(8,128)} %constant.2.clone.table_hbm, bf16[128,1024]{1,0:T(8,128)(2,1)} %acts_ref.1, ...), custom_call_target="tpu_custom_call" | custom-call | tf_op jit(solution)/shard_map/exchange/pallas_call | solution.py:325
  45.1 2.7 %store.1 = (f32[1,1024,1024]{2,1,0:T(8,128)}, bf16[1024,1024]{1,0:T(8,128)(2,1)}) custom-call(f32[4,1024,256]{2,1,0:T(8,128)S(1)} %get-tuple-element.7.residual_ref, bf16[4,1024,256]{2,1,0:T(8,128)(2,1)S(1)} %get-tuple-element.8.update_ref, f32[16,128]{1,0:T(8,128)S(1)} %get-tuple-element.9.total_ref, f32[128,256]{1,0:T(8,128)S(1)} %get-tuple-element.10.right_ref, ...), custom_call_target="tpu_custom_call" | custom-call | tf_op jit(solution)/shard_map/store/pallas_call | solution.py:361

commit v2 on v1

--- a/solution.py
+++ b/solution.py
@@ -110,14 +110,15 @@
             device_id_type=MESH,
         )
 
-    def start_grads(j):
-        for own, order in ((0, offsets), (1, offsets[::-1])):
+    def start_grads(j, some):
+        for own, order in ((0, some), (1, some[::-1])):
             @pl.when(core == own)
             def _():
                 for c in order:
                     send_grads(2 * c, j).start()
                     send_grads(2 * c + 1, j).start()
-                send_grads(1, j).start()
+        if 1 in some:
+            send_grads(1, j).start()
 
     def acts_copy(source, slot, bits, low, count, sem):
         return pltpu.make_async_remote_copy(
@@ -150,18 +151,21 @@
             device_id_type=MESH,
         )
 
+    direct = [c for c in offsets if not (square and c == 3)]
+    across = [c for c in offsets if c not in direct]
+    pl.semaphore_wait(barrier, shards - 1 + reps - 1)
+    start_grads(0, across)
     load_acts.wait()
     acts_t[:, pl.ds(0, tok)] = own_acts[...].T
-    pl.semaphore_wait(barrier, shards - 1 + reps - 1)
-
-    direct = [c for c in offsets if not (square and c == 3)]
     for own, order in ((0, direct), (1, direct[::-1])):
         @pl.when(core == own)
         def _():
             for c in order:
                 send_direct(2 * c).start()
     send_sibling(0).start()
-    start_grads(0)
+    start_grads(0, direct)
+    for j in range(1, min(2, chunks)):
+        start_grads(j, offsets)
     for j in range(chunks):
         own_grads(j).start()
         load_momentum(j).start()
@@ -198,15 +202,15 @@
                 if square:
                     send_across(6 - 2 * c).start()
                 send_sibling(2 * c).start()
-    ahead = min(3, chunks)
-    for j in range(1, min(2, chunks)):
-        start_grads(j)
+    ahead = min(4, chunks)
+    for j in range(2, min(3, chunks)):
+        start_grads(j, offsets)
     if square:
         send_across(4).wait_recv()
         send_across(2).wait_recv()
         send_sibling(6).start()
-    for j in range(2, ahead):
-        start_grads(j)
+    for j in range(3, ahead):
+        start_grads(j, offsets)
     for o in range(0, shards, 2):
         send_sibling(o).wait_recv()
 
@@ -234,7 +238,7 @@
 
         @pl.when(j + ahead < chunks)
         def _():
-            start_grads(j + ahead)
+            start_grads(j + ahead, offsets)
 
         own_grads(j).wait()
         load_momentum(j).wait()

time: 48 us -> 48.2 us (level)
  no operation moved by 1% of the time
where the time goes in v2:
time: 48.2 us; the launch traced here: 48.1 us
  Pallas kernels  47.4 us (98%)
  between operations  0.64 us (1%)
    pallas_call x1, Pallas kernels, on_device(): pl.pallas_call(functools.partial(exchange_kernel, shards, reps, chunks, k...  44.7 us
    pallas_call x1, Pallas kernels, on_device(): pl.pallas_call(store_kernel, out_shape=(jax.ShapeDtypeStruct((1, rows, co...  2.74 us

profile of v2, /device:TPU:0, one launch (start us, length us, event | category | flops | bytes accessed | tf_op | source)
XLA Modules:
  0.0 48.1 jit_solution(13172759030864550109)
XLA Ops:
  0.6 44.7 %exchange.1 = (f32[4,1024,256]{2,1,0:T(8,128)S(1)}, bf16[4,1024,256]{2,1,0:T(8,128)(2,1)S(1)}, f32[16,128]{1,0:T(8,128)S(1)}, f32[128,256]{1,0:T(8,128)S(1)}, f32[64,128]{1,0:T(8,128)S(1)}) custom-call(s32[32]{0:T(128)} %kept_hbm.1, f32[64,384]{1,0:T(8,128)} %constant.2.clone.table_hbm, bf16[128,1024]{1,0:T(8,128)(2,1)} %acts_ref.1, ...), custom_call_target="tpu_custom_call" | custom-call | tf_op jit(solution)/shard_map/exchange/pallas_call | solution.py:329
  45.3 2.7 %store.1 = (f32[1,1024,1024]{2,1,0:T(8,128)}, bf16[1024,1024]{1,0:T(8,128)(2,1)}) custom-call(f32[4,1024,256]{2,1,0:T(8,128)S(1)} %get-tuple-element.7.residual_ref, bf16[4,1024,256]{2,1,0:T(8,128)(2,1)S(1)} %get-tuple-element.8.update_ref, f32[16,128]{1,0:T(8,128)S(1)} %get-tuple-element.9.total_ref, f32[128,256]{1,0:T(8,128)S(1)} %get-tuple-element.10.right_ref, ...), custom_call_target="tpu_custom_call" | custom-call | tf_op jit(solution)/shard_map/store/pallas_call | solution.py:365

commit v3 on v2

--- a/solution.py
+++ b/solution.py
@@ -57,7 +57,7 @@
     shards, reps, chunks, kept_count,
     kept_hbm, table_hbm, acts_ref, grads_ref, momentum_ref,
     residual_ref, update_ref, total_ref, right_ref, left_ref,
-    kept_ref, table, own_acts, acts_t, grads_all, coeffs, gathered,
+    kept_ref, table, acts_all, acts_t, grads_all, coeffs, gathered,
     acts_send, acts_recv, grads_send, grads_recv, rep_send, rep_recv,
     local_kept, local_table, local_acts, local_grads, local_mom,
 ):
@@ -72,7 +72,7 @@
     square = chips == 4
     offsets = sorted(range(1, chips), key=lambda c: c == 2)
 
-    load_acts = pltpu.make_async_copy(acts_ref, own_acts, local_acts)
+    load_acts = pltpu.make_async_copy(acts_ref, acts_all.at[pl.ds(0, tok), :], local_acts)
     load_kept = pltpu.make_async_copy(kept_hbm, kept_ref, local_kept)
     load_table = pltpu.make_async_copy(table_hbm, table, local_table)
     load_acts.start()
@@ -121,9 +121,10 @@
             send_grads(1, j).start()
 
     def acts_copy(source, slot, bits, low, count, sem):
+        own = acts_ref if source == 0 else acts_all.at[pl.ds(source * tok, tok), :]
         return pltpu.make_async_remote_copy(
-            src_ref=acts_t.at[pl.ds(low, count), pl.ds(source * tok, tok)],
-            dst_ref=acts_t.at[pl.ds(low, count), pl.ds(slot * tok, tok)],
+            src_ref=own.at[pl.ds(low, count), :],
+            dst_ref=acts_all.at[pl.ds(slot * tok + low, count), :],
             send_sem=acts_send.at[sem],
             recv_sem=acts_recv.at[sem],
             device_id=(rep, flip(me, bits)),
@@ -131,15 +132,18 @@
         )
 
     def send_direct(o):
-        return acts_copy(0, o, o, 0, rows, o)
+        return acts_copy(0, o, o, 0, tok, o)
 
     def send_sibling(o):
-        return acts_copy(o, o + 1, 1, 0, rows, o + 1)
+        return acts_copy(o, o + 1, 1, 0, tok, o + 1)
+
+    def turn(o):
+        acts_t[:, pl.ds(o * tok, tok)] = acts_all[pl.ds(o * tok, tok), :].T
 
     def send_across(bits):
         if bits == 2:
-            return acts_copy(4, 6, 2, rows // 2, rows // 2, shards)
-        return acts_copy(2, 6, 4, 0, rows // 2, 6)
+            return acts_copy(4, 6, 2, tok // 2, tok // 2, shards)
+        return acts_copy(2, 6, 4, 0, tok // 2, 6)
 
     def send_coeffs(q, j):
         return pltpu.make_async_remote_copy(
@@ -152,19 +156,14 @@
         )
 
     direct = [c for c in offsets if not (square and c == 3)]
-    across = [c for c in offsets if c not in direct]
     pl.semaphore_wait(barrier, shards - 1 + reps - 1)
-    start_grads(0, across)
-    load_acts.wait()
-    acts_t[:, pl.ds(0, tok)] = own_acts[...].T
     for own, order in ((0, direct), (1, direct[::-1])):
         @pl.when(core == own)
         def _():
             for c in order:
                 send_direct(2 * c).start()
     send_sibling(0).start()
-    start_grads(0, direct)
-    for j in range(1, min(2, chunks)):
+    for j in range(min(2, chunks)):
         start_grads(j, offsets)
     for j in range(chunks):
         own_grads(j).start()
@@ -194,6 +193,8 @@
         table[:, WIDTH:WIDTH + GROUP], hot_u, precision=lax.Precision.HIGHEST, preferred_element_type=jnp.float32
     )
 
+    load_acts.wait()
+    turn(0)
     for own, order in ((0, direct), (1, direct[::-1])):
         @pl.when(core == own)
         def _():
@@ -205,14 +206,22 @@
     ahead = min(4, chunks)
     for j in range(2, min(3, chunks)):
         start_grads(j, offsets)
+    for c in direct:
+        turn(2 * c)
+    for o in range(0, shards, 2):
+        if not (square and o == 6):
+            send_sibling(o).wait_recv()
+            turn(o + 1)
     if square:
         send_across(4).wait_recv()
         send_across(2).wait_recv()
         send_sibling(6).start()
     for j in range(3, ahead):
         start_grads(j, offsets)
-    for o in range(0, shards, 2):
-        send_sibling(o).wait_recv()
+    if square:
+        turn(6)
+        send_sibling(6).wait_recv()
+        turn(7)
 
     half = rows // 2
     bands = half // GROUP
@@ -340,7 +349,7 @@
         scratch_shapes=[
             pltpu.SMEM((kept_count,), jnp.int32),
             pltpu.VMEM(table.shape, f32),
-            pltpu.VMEM((tok, rows), jnp.bfloat16),
+            pltpu.VMEM((shards * tok, rows), jnp.bfloat16),
             pltpu.VMEM((rows, shards * tok), jnp.bfloat16),
             pltpu.VMEM((chunks, shards * tok, WIDTH), jnp.bfloat16),
             pltpu.VMEM((chunks, bands, lanes), f32),

time: 48.2 us -> 48.6 us (level)
  Pallas kernels: 47.4 us -> 47.9 us
where the time goes in v3:
time: 48.6 us; the launch traced here: 48.5 us
  Pallas kernels  47.9 us (99%)
  between operations  0.64 us (1%)
    pallas_call x1, Pallas kernels, on_device(): pl.pallas_call(functools.partial(exchange_kernel, shards, reps, chunks, k...  45.1 us
    pallas_call x1, Pallas kernels, on_device(): pl.pallas_call(store_kernel, out_shape=(jax.ShapeDtypeStruct((1, rows, co...  2.74 us

profile of v3, /device:TPU:0, one launch (start us, length us, event | category | flops | bytes accessed | tf_op | source)
XLA Modules:
  0.0 48.5 jit_solution(18320683376806680846)
XLA Ops:
  0.6 45.1 %exchange.1 = (f32[4,1024,256]{2,1,0:T(8,128)S(1)}, bf16[4,1024,256]{2,1,0:T(8,128)(2,1)S(1)}, f32[16,128]{1,0:T(8,128)S(1)}, f32[128,256]{1,0:T(8,128)S(1)}, f32[64,128]{1,0:T(8,128)S(1)}) custom-call(s32[32]{0:T(128)} %kept_hbm.1, f32[64,384]{1,0:T(8,128)} %constant.2.clone.table_hbm, bf16[128,1024]{1,0:T(8,128)(2,1)} %acts_ref.1, ...), custom_call_target="tpu_custom_call" | custom-call | tf_op jit(solution)/shard_map/exchange/pallas_call | solution.py:338
  45.8 2.7 %store.1 = (f32[1,1024,1024]{2,1,0:T(8,128)}, bf16[1024,1024]{1,0:T(8,128)(2,1)}) custom-call(f32[4,1024,256]{2,1,0:T(8,128)S(1)} %get-tuple-element.7.residual_ref, bf16[4,1024,256]{2,1,0:T(8,128)(2,1)S(1)} %get-tuple-element.8.update_ref, f32[16,128]{1,0:T(8,128)S(1)} %get-tuple-element.9.total_ref, f32[128,256]{1,0:T(8,128)S(1)} %get-tuple-element.10.right_ref, ...), custom_call_target="tpu_custom_call" | custom-call | tf_op jit(solution)/shard_map/store/pallas_call | solution.py:374

commit v4 on v3

--- a/solution.py
+++ b/solution.py
@@ -59,7 +59,7 @@
     residual_ref, update_ref, total_ref, right_ref, left_ref,
     kept_ref, table, acts_all, acts_t, grads_all, coeffs, gathered,
     acts_send, acts_recv, grads_send, grads_recv, rep_send, rep_recv,
-    local_kept, local_table, local_acts, local_grads, local_mom,
+    local_kept, local_table, local_acts, local_grads, local_mom, transit, transit_send, transit_recv,
 ):
     rep = lax.axis_index("rep")
     me = lax.axis_index("shard")
@@ -70,7 +70,8 @@
     lanes = tiles * kept_count
     chips = shards // 2
     square = chips == 4
-    offsets = sorted(range(1, chips), key=lambda c: c == 2)
+    direct = [c for c in range(1, chips) if not (square and c == 3)]
+    straight = [1] + [2 * c + b for c in direct for b in range(2)]
 
     load_acts = pltpu.make_async_copy(acts_ref, acts_all.at[pl.ds(0, tok), :], local_acts)
     load_kept = pltpu.make_async_copy(kept_hbm, kept_ref, local_kept)
@@ -114,11 +115,47 @@
         for own, order in ((0, some), (1, some[::-1])):
             @pl.when(core == own)
             def _():
+                if square:
+                    for c in order:
+                        for b in range(2):
+                            first_hop(c, b, j).start()
                 for c in order:
                     send_grads(2 * c, j).start()
                     send_grads(2 * c + 1, j).start()
-        if 1 in some:
-            send_grads(1, j).start()
+        send_grads(1, j).start()
+
+    def first_hop(c, b, j):
+        peer = flip(me, 6 + b)
+        column = pl.multiple_of(peer * columns + j * WIDTH, WIDTH)
+        return pltpu.make_async_remote_copy(
+            src_ref=grads_ref.at[pl.ds((c - 1) * (tok // 2), tok // 2), pl.ds(column, WIDTH)],
+            dst_ref=transit.at[j, c - 1, b],
+            send_sem=transit_send.at[j, c - 1, b],
+            recv_sem=transit_recv.at[j, c - 1, b],
+            device_id=(rep, flip(me, 2 * c)),
+            device_id_type=MESH,
+        )
+
+    def second_hop(c, b, j):
+        return pltpu.make_async_remote_copy(
+            src_ref=transit.at[j, c - 1, b],
+            dst_ref=grads_all.at[j, pl.ds((6 + b) * tok + (c - 1) * (tok // 2), tok // 2), :],
+            send_sem=grads_send.at[j, 6 + b + 2 * (c - 1)],
+            recv_sem=grads_recv.at[j, 6 + b + 2 * (c - 1)],
+            device_id=(rep, flip(me, 6 - 2 * c + b)),
+            device_id_type=MESH,
+        )
+
+    def hand_on(j):
+        for own, order in ((0, direct), (1, direct[::-1])):
+            @pl.when(core == own)
+            def _():
+                for c in order:
+                    for b in range(2):
+                        first_hop(c, b, j).wait_recv()
+                        second_hop(c, b, j).start()
+
+    hops = [(c, b) for c in (1, 2) for b in range(2)] if square else []
 
     def acts_copy(source, slot, bits, low, count, sem):
         own = acts_ref if source == 0 else acts_all.at[pl.ds(source * tok, tok), :]
@@ -155,7 +192,6 @@
             device_id_type=MESH,
         )
 
-    direct = [c for c in offsets if not (square and c == 3)]
     pl.semaphore_wait(barrier, shards - 1 + reps - 1)
     for own, order in ((0, direct), (1, direct[::-1])):
         @pl.when(core == own)
@@ -164,7 +200,7 @@
                 send_direct(2 * c).start()
     send_sibling(0).start()
     for j in range(min(2, chunks)):
-        start_grads(j, offsets)
+        start_grads(j, direct)
     for j in range(chunks):
         own_grads(j).start()
         load_momentum(j).start()
@@ -205,7 +241,7 @@
                 send_sibling(2 * c).start()
     ahead = min(4, chunks)
     for j in range(2, min(3, chunks)):
-        start_grads(j, offsets)
+        start_grads(j, direct)
     for c in direct:
         turn(2 * c)
     for o in range(0, shards, 2):
@@ -217,8 +253,9 @@
         send_across(2).wait_recv()
         send_sibling(6).start()
     for j in range(3, ahead):
-        start_grads(j, offsets)
+        start_grads(j, direct)
     if square:
+        hand_on(0)
         turn(6)
         send_sibling(6).wait_recv()
         turn(7)
@@ -242,12 +279,19 @@
                 ).astype(jnp.bfloat16)
 
     def chunk(j, carry):
-        for o in range(1, shards):
+        if square:
+            @pl.when(j + 1 < chunks)
+            def _():
+                hand_on(j + 1)
+
+        for o in straight:
             send_grads(o, j).wait_recv()
+        for c, b in hops:
+            second_hop(c, b, j).wait_recv()
 
         @pl.when(j + ahead < chunks)
         def _():
-            start_grads(j + ahead, offsets)
+            start_grads(j + ahead, direct)
 
         own_grads(j).wait()
         load_momentum(j).wait()
@@ -281,8 +325,11 @@
     lax.fori_loop(0, chunks, chunk, 0)
 
     def drain(j, carry):
-        for o in range(1, shards):
+        for o in straight:
             send_grads(o, j).wait_send()
+        for c, b in hops:
+            first_hop(c, b, j).wait_send()
+            second_hop(c, b, j).wait_send()
         return carry
 
     lax.fori_loop(0, chunks, drain, 0)
@@ -356,8 +403,8 @@
             pltpu.VMEM((chunks, reps, bands, lanes), f32),
             pltpu.SemaphoreType.DMA((shards + 1,)),
             pltpu.SemaphoreType.DMA((shards + 1,)),
-            pltpu.SemaphoreType.DMA((chunks, shards)),
-            pltpu.SemaphoreType.DMA((chunks, shards)),
+            pltpu.SemaphoreType.DMA((chunks, shards + 2)),
+            pltpu.SemaphoreType.DMA((chunks, shards + 2)),
             pltpu.SemaphoreType.DMA((chunks, reps)),
             pltpu.SemaphoreType.DMA((chunks, reps)),
             pltpu.SemaphoreType.DMA,
@@ -365,6 +412,9 @@
             pltpu.SemaphoreType.DMA,
             pltpu.SemaphoreType.DMA((chunks,)),
             pltpu.SemaphoreType.DMA((chunks,)),
+            pltpu.VMEM((chunks, 2, 2, tok // 2, WIDTH), jnp.bfloat16),
+            pltpu.SemaphoreType.DMA((chunks, 2, 2)),
+            pltpu.SemaphoreType.DMA((chunks, 2, 2)),
         ],
         compiler_params=pltpu.CompilerParams(
             collective_id=0, has_side_effects=True, vmem_limit_bytes=40 * 2**20

time: 48.6 us -> 54.2 us (1.12)
  Pallas kernels: 47.9 us -> 53.4 us
    pallas_call x1, Pallas kernels: 45.1 us -> 50.7 us  [on_device(): pl.pallas_call(functools.partial(exchange_kernel, shards, reps, chunks, k...]
where the time goes in v4:
time: 54.2 us; the launch traced here: 54.1 us
  Pallas kernels  53.4 us (99%)
  between operations  0.64 us (1%)
    pallas_call x1, Pallas kernels, on_device(): pl.pallas_call(functools.partial(exchange_kernel, shards, reps, chunks, k...  50.7 us
    pallas_call x1, Pallas kernels, on_device(): pl.pallas_call(store_kernel, out_shape=(jax.ShapeDtypeStruct((1, rows, co...  2.74 us

profile of v4, /device:TPU:0, one launch (start us, length us, event | category | flops | bytes accessed | tf_op | source)
XLA Modules:
  0.0 54.1 jit_solution(10813643723648921652)
XLA Ops:
  0.6 50.7 %exchange.1 = (f32[4,1024,256]{2,1,0:T(8,128)S(1)}, bf16[4,1024,256]{2,1,0:T(8,128)(2,1)S(1)}, f32[16,128]{1,0:T(8,128)S(1)}, f32[128,256]{1,0:T(8,128)S(1)}, f32[64,128]{1,0:T(8,128)S(1)}) custom-call(s32[32]{0:T(128)} %kept_hbm.1, f32[64,384]{1,0:T(8,128)} %constant.2.clone.table_hbm, bf16[128,1024]{1,0:T(8,128)(2,1)} %acts_ref.1, ...), custom_call_target="tpu_custom_call" | custom-call | tf_op jit(solution)/shard_map/exchange/pallas_call | solution.py:385
  51.3 2.7 %store.1 = (f32[1,1024,1024]{2,1,0:T(8,128)}, bf16[1024,1024]{1,0:T(8,128)(2,1)}) custom-call(f32[4,1024,256]{2,1,0:T(8,128)S(1)} %get-tuple-element.7.residual_ref, bf16[4,1024,256]{2,1,0:T(8,128)(2,1)S(1)} %get-tuple-element.8.update_ref, f32[16,128]{1,0:T(8,128)S(1)} %get-tuple-element.9.total_ref, f32[128,256]{1,0:T(8,128)S(1)} %get-tuple-element.10.right_ref, ...), custom_call_target="tpu_custom_call" | custom-call | tf_op jit(solution)/shard_map/store/pallas_call | solution.py:424

commit v5 on v3

--- a/solution.py
+++ b/solution.py
@@ -11,6 +11,7 @@
 
 GROUP = 64
 WIDTH = 256
+SPAN = 512
 DECAY = 0.9
 MESH = pl.DeviceIdType.MESH
 
@@ -66,6 +67,9 @@
     core = me % 2
     tok, rows = acts_ref.shape
     columns = chunks * WIDTH
+    span = min(SPAN, columns)
+    parts = span // WIDTH
+    spans = columns // span
     tiles = WIDTH // GROUP
     lanes = tiles * kept_count
     chips = shards // 2
@@ -87,7 +91,7 @@
 
     def own_grads(j):
         return pltpu.make_async_copy(
-            grads_ref.at[:, pl.ds(pl.multiple_of(me * columns + j * WIDTH, WIDTH), WIDTH)],
+            grads_ref.at[:, pl.ds(pl.multiple_of(me * columns + j * span, span), span)],
             grads_all.at[j, pl.ds(0, tok), :],
             local_grads.at[j],
         )
@@ -102,7 +106,7 @@
     def send_grads(o, j):
         peer = flip(me, o)
         return pltpu.make_async_remote_copy(
-            src_ref=grads_ref.at[:, pl.ds(pl.multiple_of(peer * columns + j * WIDTH, WIDTH), WIDTH)],
+            src_ref=grads_ref.at[:, pl.ds(pl.multiple_of(peer * columns + j * span, span), span)],
             dst_ref=grads_all.at[j, pl.ds(o * tok, tok), :],
             send_sem=grads_send.at[j, o],
             recv_sem=grads_recv.at[j, o],
@@ -163,10 +167,11 @@
             for c in order:
                 send_direct(2 * c).start()
     send_sibling(0).start()
-    for j in range(min(2, chunks)):
-        start_grads(j, offsets)
+    ahead = min(2, spans)
+    start_grads(0, offsets)
+    for j in range(spans):
+        own_grads(j).start()
     for j in range(chunks):
-        own_grads(j).start()
         load_momentum(j).start()
 
     load_kept.wait()
@@ -203,8 +208,7 @@
                 if square:
                     send_across(6 - 2 * c).start()
                 send_sibling(2 * c).start()
-    ahead = min(4, chunks)
-    for j in range(2, min(3, chunks)):
+    for j in range(1, ahead):
         start_grads(j, offsets)
     for c in direct:
         turn(2 * c)
@@ -216,8 +220,6 @@
         send_across(4).wait_recv()
         send_across(2).wait_recv()
         send_sibling(6).start()
-    for j in range(3, ahead):
-        start_grads(j, offsets)
     if square:
         turn(6)
         send_sibling(6).wait_recv()
@@ -226,66 +228,70 @@
     half = rows // 2
     bands = half // GROUP
 
-    def finish(j, with_update):
+    def add_replicas(j):
         for q in range(1, reps):
             send_coeffs(q, j).wait_recv()
         terms = [coeffs[j]] + [gathered[j, q] for q in range(1, reps)]
         while len(terms) > 1:
             terms = [terms[i] + terms[i + 1] for i in range(0, len(terms), 2)]
-        total_ref[...] = terms[0]
-        if with_update:
-            right_high, right_low = split(right_ref[...])
-            for t in range(2):
-                values = total_ref[pl.ds(t * bands, bands), :]
-                update_ref[j, pl.ds(t * half, half), :] = decode(
-                    values, left_ref[...], right_high, right_low
-                ).astype(jnp.bfloat16)
-
-    def chunk(j, carry):
+        return terms[0]
+
+    def columns_span(i, carry):
         for o in range(1, shards):
-            send_grads(o, j).wait_recv()
-
-        @pl.when(j + ahead < chunks)
+            send_grads(o, i).wait_recv()
+
+        @pl.when(i + ahead < spans)
         def _():
-            start_grads(j + ahead, offsets)
-
-        own_grads(j).wait()
-        load_momentum(j).wait()
+            start_grads(i + ahead, offsets)
+
+        own_grads(i).wait()
         right_high, right_low = split(right_ref[...])
         right_both = jnp.concatenate([right_high, right_low], axis=0)
         left = left_ref[...]
-        for t in range(2):
-            part = pl.ds(t * half, half)
-            gradient = dot_nn(acts_t[part, :], grads_all[j])
-            value = DECAY * residual_ref[j, part, :] + gradient
-            residual_ref[j, part, :] = value
-            high, low = split(value)
-            both = dot_nt(high, right_both)
-            done = both[:, :lanes] + both[:, lanes:] + dot_nt(low, right_high)
-            coeffs[j, pl.ds(t * bands, bands), :] = jnp.sum(
-                done.reshape(bands, GROUP, lanes) * left[None], axis=1
-            )
-        for q in range(1, reps):
-            send_coeffs(q, j).start()
-        for t in range(2):
-            part = pl.ds(t * half, half)
-            values = coeffs[j, pl.ds(t * bands, bands), :]
-            residual_ref[j, part, :] = residual_ref[j, part, :] - decode(values, left, right_high, right_low)
-
-        @pl.when(j > 0)
+        for p in range(parts):
+            j = i * parts + p
+            load_momentum(j).wait()
+            for t in range(2):
+                part = pl.ds(t * half, half)
+                gradient = dot_nn(acts_t[part, :], grads_all[i, :, p * WIDTH:(p + 1) * WIDTH])
+                value = DECAY * residual_ref[j, part, :] + gradient
+                residual_ref[j, part, :] = value
+                high, low = split(value)
+                both = dot_nt(high, right_both)
+                done = both[:, :lanes] + both[:, lanes:] + dot_nt(low, right_high)
+                coeffs[j, pl.ds(t * bands, bands), :] = jnp.sum(
+                    done.reshape(bands, GROUP, lanes) * left[None], axis=1
+                )
+            for q in range(1, reps):
+                send_coeffs(q, j).start()
+        for p in range(parts):
+            j = i * parts + p
+            for t in range(2):
+                part = pl.ds(t * half, half)
+                values = coeffs[j, pl.ds(t * bands, bands), :]
+                residual_ref[j, part, :] = residual_ref[j, part, :] - decode(values, left, right_high, right_low)
+
+        @pl.when(i > 0)
         def _():
-            finish(j - 1, True)
+            for p in range(parts):
+                j = (i - 1) * parts + p
+                total_ref[0] = add_replicas(j)
+                for t in range(2):
+                    values = total_ref[0, pl.ds(t * bands, bands), :]
+                    update_ref[j, pl.ds(t * half, half), :] = decode(
+                        values, left, right_high, right_low
+                    ).astype(jnp.bfloat16)
 
         return carry
 
-    lax.fori_loop(0, chunks, chunk, 0)
+    lax.fori_loop(0, spans, columns_span, 0)
 
     def drain(j, carry):
         for o in range(1, shards):
             send_grads(o, j).wait_send()
         return carry
 
-    lax.fori_loop(0, chunks, drain, 0)
+    lax.fori_loop(0, spans, drain, 0)
     for c in direct:
         send_direct(2 * c).wait_send()
     for o in range(0, shards, 2):
@@ -293,7 +299,8 @@
     if square:
         send_across(2).wait_send()
         send_across(4).wait_send()
-    finish(chunks - 1, False)
+    for p in range(parts):
+        total_ref[p] = add_replicas((spans - 1) * parts + p)
     for j in range(chunks):
         for q in range(1, reps):
             send_coeffs(q, j).wait_send()
@@ -307,14 +314,16 @@
     def store(source, target, sem, j):
         return pltpu.make_async_copy(source, target.at[:, pl.ds(j * WIDTH, WIDTH)], sem.at[j])
 
-    copies = [store(update_ref.at[j], update_out, update_sem, j) for j in range(chunks - 1)]
-    copies += [store(residual_ref.at[j], residual_out.at[0], residual_sem, j) for j in range(chunks)]
+    parts = total_ref.shape[0]
+    copies = [store(residual_ref.at[j], residual_out.at[0], residual_sem, j) for j in range(chunks)]
+    copies += [store(update_ref.at[j], update_out, update_sem, j) for j in range(chunks - parts)]
     for copy in copies:
         copy.start()
     right_high, right_low = split(right_ref[...])
-    last[...] = decode(total_ref[...], left_ref[...], right_high, right_low).astype(jnp.bfloat16)
-    copies.append(store(last, update_out, update_sem, chunks - 1))
-    copies[-1].start()
+    for p in range(parts):
+        last[p] = decode(total_ref[p], left_ref[...], right_high, right_low).astype(jnp.bfloat16)
+        copies.append(store(last.at[p], update_out, update_sem, chunks - parts + p))
+        copies[-1].start()
     for copy in copies:
         copy.wait()
 
@@ -323,6 +332,9 @@
     tok, rows = hidden_acts.shape
     columns = momentum.shape[2]
     chunks = columns // WIDTH
+    span = min(SPAN, columns)
+    spans = columns // span
+    parts = span // WIDTH
     kept_count = kept.shape[0]
     tiles = WIDTH // GROUP
     lanes = tiles * kept_count
@@ -340,7 +352,7 @@
         out_shape=(
             jax.ShapeDtypeStruct((chunks, rows, WIDTH), f32),
             jax.ShapeDtypeStruct((chunks, rows, WIDTH), jnp.bfloat16),
-            jax.ShapeDtypeStruct((bands, lanes), f32),
+            jax.ShapeDtypeStruct((parts, bands, lanes), f32),
             jax.ShapeDtypeStruct((lanes, WIDTH), f32),
             jax.ShapeDtypeStruct((GROUP, lanes), f32),
         ),
@@ -351,13 +363,13 @@
             pltpu.VMEM(table.shape, f32),
             pltpu.VMEM((shards * tok, rows), jnp.bfloat16),
             pltpu.VMEM((rows, shards * tok), jnp.bfloat16),
-            pltpu.VMEM((chunks, shards * tok, WIDTH), jnp.bfloat16),
+            pltpu.VMEM((spans, shards * tok, span), jnp.bfloat16),
             pltpu.VMEM((chunks, bands, lanes), f32),
             pltpu.VMEM((chunks, reps, bands, lanes), f32),
             pltpu.SemaphoreType.DMA((shards + 1,)),
             pltpu.SemaphoreType.DMA((shards + 1,)),
-            pltpu.SemaphoreType.DMA((chunks, shards)),
-            pltpu.SemaphoreType.DMA((chunks, shards)),
+            pltpu.SemaphoreType.DMA((spans, shards)),
+            pltpu.SemaphoreType.DMA((spans, shards)),
             pltpu.SemaphoreType.DMA((chunks, reps)),
             pltpu.SemaphoreType.DMA((chunks, reps)),
             pltpu.SemaphoreType.DMA,
@@ -380,7 +392,7 @@
         in_specs=[vmem] * 5,
         out_specs=(hbm, hbm),
         scratch_shapes=[
-            pltpu.VMEM((rows, WIDTH), jnp.bfloat16),
+            pltpu.VMEM((parts, rows, WIDTH), jnp.bfloat16),
             pltpu.SemaphoreType.DMA((chunks,)),
             pltpu.SemaphoreType.DMA((chunks,)),
         ],

time: 48.6 us -> 49.5 us (1.019)
  Pallas kernels: 47.9 us -> 48.7 us
    pallas_call x1, Pallas kernels: 45.1 us -> 46 us  [on_device(): pl.pallas_call(functools.partial(exchange_kernel, shards, reps, chunks, k...]
where the time goes in v5:
time: 49.5 us; the launch traced here: 49.4 us
  Pallas kernels  48.7 us (98%)
  between operations  0.64 us (1%)
    pallas_call x1, Pallas kernels, on_device(): pl.pallas_call(functools.partial(exchange_kernel, shards, reps, chunks, k...  46 us
    pallas_call x1, Pallas kernels, on_device(): pl.pallas_call(store_kernel, out_shape=(jax.ShapeDtypeStruct((1, rows, co...  2.72 us

profile of v5, /device:TPU:0, one launch (start us, length us, event | category | flops | bytes accessed | tf_op | source)
XLA Modules:
  0.0 49.4 jit_solution(16359299586289096189)
XLA Ops:
  0.6 46.0 %exchange.1 = (f32[4,1024,256]{2,1,0:T(8,128)S(1)}, bf16[4,1024,256]{2,1,0:T(8,128)(2,1)S(1)}, f32[2,16,128]{2,1,0:T(8,128)S(1)}, f32[128,256]{1,0:T(8,128)S(1)}, f32[64,128]{1,0:T(8,128)S(1)}) custom-call(s32[32]{0:T(128)} %kept_hbm.1, f32[64,384]{1,0:T(8,128)} %constant.2.clone.table_hbm, bf16[128,1024]{1,0:T(8,128)(2,1)} %acts_ref.1, ...), custom_call_target="tpu_custom_call" | custom-call | tf_op jit(solution)/shard_map/exchange/pallas_call | solution.py:350
  46.7 2.7 %store.1 = (f32[1,1024,1024]{2,1,0:T(8,128)}, bf16[1024,1024]{1,0:T(8,128)(2,1)}) custom-call(f32[4,1024,256]{2,1,0:T(8,128)S(1)} %get-tuple-element.7.residual_ref, bf16[4,1024,256]{2,1,0:T(8,128)(2,1)S(1)} %get-tuple-element.8.update_ref, f32[2,16,128]{2,1,0:T(8,128)S(1)} %get-tuple-element.9.total_ref, f32[128,256]{1,0:T(8,128)S(1)} %get-tuple-element.10.right_ref, ...), custom_call_target="tpu_custom_call" | custom-call | tf_op jit(solution)/shard_map/store/pallas_call | solution.py:386

commit v6 on v3

--- a/solution.py
+++ b/solution.py
@@ -111,14 +111,12 @@
         )
 
     def start_grads(j, some):
-        for own, order in ((0, some), (1, some[::-1])):
+        turns = [2 * c for c in some] + [1] + [2 * c + 1 for c in some]
+        for own, order in ((0, turns), (1, turns[::-1])):
             @pl.when(core == own)
             def _():
-                for c in order:
-                    send_grads(2 * c, j).start()
-                    send_grads(2 * c + 1, j).start()
-        if 1 in some:
-            send_grads(1, j).start()
+                for o in order:
+                    send_grads(o, j).start()
 
     def acts_copy(source, slot, bits, low, count, sem):
         own = acts_ref if source == 0 else acts_all.at[pl.ds(source * tok, tok), :]
@@ -163,8 +161,7 @@
             for c in order:
                 send_direct(2 * c).start()
     send_sibling(0).start()
-    for j in range(min(2, chunks)):
-        start_grads(j, offsets)
+    start_grads(0, offsets)
     for j in range(chunks):
         own_grads(j).start()
         load_momentum(j).start()
@@ -203,8 +200,8 @@
                 if square:
                     send_across(6 - 2 * c).start()
                 send_sibling(2 * c).start()
-    ahead = min(4, chunks)
-    for j in range(2, min(3, chunks)):
+    ahead = min(3, chunks)
+    for j in range(1, min(2, chunks)):
         start_grads(j, offsets)
     for c in direct:
         turn(2 * c)
@@ -216,7 +213,7 @@
         send_across(4).wait_recv()
         send_across(2).wait_recv()
         send_sibling(6).start()
-    for j in range(3, ahead):
+    for j in range(2, ahead):
         start_grads(j, offsets)
     if square:
         turn(6)

time: 48.6 us -> 46.9 us (0.965)
  Pallas kernels: 47.9 us -> 46.1 us
    pallas_call x1, Pallas kernels: 45.1 us -> 43.3 us  [on_device(): pl.pallas_call(functools.partial(exchange_kernel, shards, reps, chunks, k...]
where the time goes in v6:
time: 46.9 us; the launch traced here: 46.7 us
  Pallas kernels  46.1 us (98%)
  between operations  0.64 us (1%)
    pallas_call x1, Pallas kernels, on_device(): pl.pallas_call(functools.partial(exchange_kernel, shards, reps, chunks, k...  43.3 us
    pallas_call x1, Pallas kernels, on_device(): pl.pallas_call(store_kernel, out_shape=(jax.ShapeDtypeStruct((1, rows, co...  2.74 us

profile of v6, /device:TPU:0, one launch (start us, length us, event | category | flops | bytes accessed | tf_op | source)
XLA Modules:
  0.0 46.7 jit_solution(10201466434378796267)
XLA Ops:
  0.6 43.3 %exchange.1 = (f32[4,1024,256]{2,1,0:T(8,128)S(1)}, bf16[4,1024,256]{2,1,0:T(8,128)(2,1)S(1)}, f32[16,128]{1,0:T(8,128)S(1)}, f32[128,256]{1,0:T(8,128)S(1)}, f32[64,128]{1,0:T(8,128)S(1)}) custom-call(s32[32]{0:T(128)} %kept_hbm.1, f32[64,384]{1,0:T(8,128)} %constant.2.clone.table_hbm, bf16[128,1024]{1,0:T(8,128)(2,1)} %acts_ref.1, ...), custom_call_target="tpu_custom_call" | custom-call | tf_op jit(solution)/shard_map/exchange/pallas_call | solution.py:335
  44.0 2.7 %store.1 = (f32[1,1024,1024]{2,1,0:T(8,128)}, bf16[1024,1024]{1,0:T(8,128)(2,1)}) custom-call(f32[4,1024,256]{2,1,0:T(8,128)S(1)} %get-tuple-element.7.residual_ref, bf16[4,1024,256]{2,1,0:T(8,128)(2,1)S(1)} %get-tuple-element.8.update_ref, f32[16,128]{1,0:T(8,128)S(1)} %get-tuple-element.9.total_ref, f32[128,256]{1,0:T(8,128)S(1)} %get-tuple-element.10.right_ref, ...), custom_call_target="tpu_custom_call" | custom-call | tf_op jit(solution)/shard_map/store/pallas_call | solution.py:371

commit v7 on v6

--- a/solution.py
+++ b/solution.py
@@ -129,8 +129,8 @@
             device_id_type=MESH,
         )
 
-    def send_direct(o):
-        return acts_copy(0, o, o, 0, tok, o)
+    def send_direct(o, part):
+        return acts_copy(0, o, o, part * (tok // 2), tok // 2, o + part * (shards + 1))
 
     def send_sibling(o):
         return acts_copy(o, o + 1, 1, 0, tok, o + 1)
@@ -158,8 +158,9 @@
     for own, order in ((0, direct), (1, direct[::-1])):
         @pl.when(core == own)
         def _():
-            for c in order:
-                send_direct(2 * c).start()
+            for part in range(2):
+                for c in order:
+                    send_direct(2 * c, part).start()
     send_sibling(0).start()
     start_grads(0, offsets)
     for j in range(chunks):
@@ -196,7 +197,8 @@
         @pl.when(core == own)
         def _():
             for c in order:
-                send_direct(2 * c).wait_recv()
+                send_direct(2 * c, 0).wait_recv()
+                send_direct(2 * c, 1).wait_recv()
                 if square:
                     send_across(6 - 2 * c).start()
                 send_sibling(2 * c).start()
@@ -284,7 +286,8 @@
 
     lax.fori_loop(0, chunks, drain, 0)
     for c in direct:
-        send_direct(2 * c).wait_send()
+        send_direct(2 * c, 0).wait_send()
+        send_direct(2 * c, 1).wait_send()
     for o in range(0, shards, 2):
         send_sibling(o).wait_send()
     if square:
@@ -351,8 +354,8 @@
             pltpu.VMEM((chunks, shards * tok, WIDTH), jnp.bfloat16),
             pltpu.VMEM((chunks, bands, lanes), f32),
             pltpu.VMEM((chunks, reps, bands, lanes), f32),
-            pltpu.SemaphoreType.DMA((shards + 1,)),
-            pltpu.SemaphoreType.DMA((shards + 1,)),
+            pltpu.SemaphoreType.DMA((2 * shards + 1,)),
+            pltpu.SemaphoreType.DMA((2 * shards + 1,)),
             pltpu.SemaphoreType.DMA((chunks, shards)),
             pltpu.SemaphoreType.DMA((chunks, shards)),
             pltpu.SemaphoreType.DMA((chunks, reps)),

time: 46.9 us -> 47.1 us (level)
  no operation moved by 1% of the time
where the time goes in v7:
time: 47.1 us; the launch traced here: 46.8 us
  Pallas kernels  46.2 us (98%)
  between operations  0.64 us (1%)
    pallas_call x1, Pallas kernels, on_device(): pl.pallas_call(functools.partial(exchange_kernel, shards, reps, chunks, k...  43.5 us
    pallas_call x1, Pallas kernels, on_device(): pl.pallas_call(store_kernel, out_shape=(jax.ShapeDtypeStruct((1, rows, co...  2.74 us

profile of v7, /device:TPU:0, one launch (start us, length us, event | category | flops | bytes accessed | tf_op | source)
XLA Modules:
  0.0 46.8 jit_solution(11738207397653527988)
XLA Ops:
  0.6 43.5 %exchange.1 = (f32[4,1024,256]{2,1,0:T(8,128)S(1)}, bf16[4,1024,256]{2,1,0:T(8,128)(2,1)S(1)}, f32[16,128]{1,0:T(8,128)S(1)}, f32[128,256]{1,0:T(8,128)S(1)}, f32[64,128]{1,0:T(8,128)S(1)}) custom-call(s32[32]{0:T(128)} %kept_hbm.1, f32[64,384]{1,0:T(8,128)} %constant.2.clone.table_hbm, bf16[128,1024]{1,0:T(8,128)(2,1)} %acts_ref.1, ...), custom_call_target="tpu_custom_call" | custom-call | tf_op jit(solution)/shard_map/exchange/pallas_call | solution.py:338
  44.1 2.7 %store.1 = (f32[1,1024,1024]{2,1,0:T(8,128)}, bf16[1024,1024]{1,0:T(8,128)(2,1)}) custom-call(f32[4,1024,256]{2,1,0:T(8,128)S(1)} %get-tuple-element.7.residual_ref, bf16[4,1024,256]{2,1,0:T(8,128)(2,1)S(1)} %get-tuple-element.8.update_ref, f32[16,128]{1,0:T(8,128)S(1)} %get-tuple-element.9.total_ref, f32[128,256]{1,0:T(8,128)S(1)} %get-tuple-element.10.right_ref, ...), custom_call_target="tpu_custom_call" | custom-call | tf_op jit(solution)/shard_map/store/pallas_call | solution.py:374
